TPU v7x, 128 devices: a whole 4x4x4 slice. The times are simulated.
128 devices in a mesh: rows: 32 (over y, z, core), cols: 4 (over x).
Axes of the slice: x: 4, y: 4, z: 4, core: 2. Of those that a mesh axis runs over, the one named last changes fastest.
Arguments:
- points: float32 [16, 1048576], P(None, ('rows', 'cols')), may hold values from -2 to 2
- coeffs: float32 [32, 1048576], P(None, ('rows', 'cols')), may hold values from -6 to 6
- velocity: float32 [32, 1048576], P(None, ('rows', 'cols')), may hold values from -4 to 4
- targets: float32 [32, 1048576], P(None, ('rows', 'cols')), may hold values from -6 to 6
- batch_index: int32 [2, 2048], replicated, may hold values from 0 to 1048575, as said below
- test_points: float32 [16, 4096], P(None, 'cols'), may hold values from -2 to 2
Outputs:
- coeffs_out: float32 [32, 1048576], P(None, ('rows', 'cols'))
- velocity_out: float32 [32, 1048576], P(None, ('rows', 'cols'))
- samples: float32 [32, 4096], P(None, 'cols')
Inputs may be any that keep to these rules, and one draw needn't show every extreme that they name: `batch_index`: row numbers of training points, 2048 in each step; a row may repeat within a step, and rows of low-numbered devices are drawn far more often than others.
All inputs are finite; a program needn't handle non-finite values.
Results may differ from a plain program's by a relative error of at most 0.0042.
Values sent between devices are 32-bit elements; how exact they have to be, the bound alone decides.
No kernel may reach another device: no remote copies, remote signals or barrier semaphores. Data moves between devices by JAX's collectives and lax.ppermute only.
A program may use at most 128 MiB of HBM per device.

v0:
```python
import math
import jax
import jax.numpy as jnp
from jax import lax
from jax.sharding import PartitionSpec as P

SCALE = 3.0**0.5 / 1.25


def matern_tile(points_block, queries):
    cross_term = jnp.dot(
        points_block.T, queries, precision=lax.Precision.HIGHEST, preferred_element_type=jnp.float32
    )
    sq_points = jnp.sum(points_block * points_block, axis=0)
    sq_queries = jnp.sum(queries * queries, axis=0)
    dist_sq = jnp.maximum(sq_points[:, None] + sq_queries[None, :] - 2.0 * cross_term, 0.0)
    scaled = SCALE * jnp.sqrt(dist_sq)
    return ((1.0 + scaled) * jnp.exp(-scaled)).astype(jnp.bfloat16)


def kernel_times(points, coeff_half, queries):
    query_count = queries.shape[1]
    blk_width = math.gcd(query_count, 512)
    blocks = queries.reshape(queries.shape[0], query_count // blk_width, blk_width).transpose(
        1, 0, 2
    )

    def apply_block(block):
        return jnp.dot(coeff_half, matern_tile(points, block), preferred_element_type=jnp.float32)

    results = lax.map(apply_block, blocks)
    return results.transpose(1, 0, 2).reshape(coeff_half.shape[0], query_count)


def per_device(points, coeffs, velocity, targets, batch_index, test_points):
    local_count = points.shape[1]
    row_start = lax.axis_index(("rows", "cols")) * local_count

    def take_owned(array, safe_rows, weights):
        return jnp.take(array, safe_rows, axis=1) * weights[None, :]

    steps_total = batch_index.shape[0]
    coeffs_now = coeffs
    velocity_now = velocity
    for step_no in range(steps_total):
        picked = batch_index[step_no]
        offset = picked - row_start
        inside = (offset >= 0) & (offset < local_count)
        owned_safe_rows = jnp.clip(offset, 0, local_count - 1)
        safe_rows = owned_safe_rows
        weights = inside.astype(jnp.float32)
        batch_points = lax.psum(take_owned(points, safe_rows, weights), ("rows", "cols"))
        partial_sums = kernel_times(points, coeffs_now.astype(jnp.bfloat16), batch_points)
        own_terms = take_owned(coeffs_now, safe_rows, weights) * 1.0 - take_owned(
            targets, safe_rows, weights
        )
        gradient = lax.psum(partial_sums + own_terms, ("rows", "cols"))
        summed = jnp.zeros_like(coeffs_now).at[:, safe_rows].add(gradient * weights[None, :])
        velocity_now = 0.9 * velocity_now - 0.5 * summed
        coeffs_now = coeffs_now + velocity_now
    coeff_half = coeffs_now.astype(jnp.bfloat16)
    partial_test = kernel_times(
        points, coeff_half, lax.all_gather(test_points, "cols", axis=1, tiled=True)
    )
    slab_sum = lax.psum_scatter(partial_test, "cols", scatter_dimension=1, tiled=True)
    slab_sum = lax.psum(slab_sum, "rows")
    return (coeffs_now, velocity_now, slab_sum)


def solution(mesh):
    return jax.shard_map(
        per_device,
        mesh=mesh,
        in_specs=(
            P(None, ("rows", "cols")),
            P(None, ("rows", "cols")),
            P(None, ("rows", "cols")),
            P(None, ("rows", "cols")),
            P(),
            P(None, "cols"),
        ),
        out_specs=(P(None, ("rows", "cols")), P(None, ("rows", "cols")), P(None, "cols")),
        check_vma=False,
    )
```

profile of v0, /device:TPU:1, one launch (start us, length us, event | category | flops | bytes accessed | tf_op | source)
XLA Modules:
  0.0 1088.0 jit_solution(15402246799207417307)
XLA Ops:
  64.4 104.7 %all-reduce.6.cloned.1.call-done = f32[4,16,512]{2,1,0:T(8,128)} async-done(((f32[4,16,512]{2,1,0:T(8,128)}), f32[4,16,512]{2,1,0:T(8,128)}) %all-reduce.6.cloned.1.call-update) | async-done | bytes 131088 | tf_op jit(solution)/shard_map/psum | solution.py:52
  169.1 109.0 %while.36 = (s32[]{:T(128)}, f32[4,32,512]{2,1,0:T(8,128)S(1)}, f32[8192]{0:T(1024)S(1)}, f32[4,16,512]{2,1,0:T(8,128)}, f32[16,8192]{1,0:T(8,128)S(1)}, /*index=5*/bf16[32,8192]{1,0:T(8,128)(2,1)S(1)}, s32[]{:T(128)}) while((s32[]{:T(128)}, f32[4,32,512]{2,1,0:T(8,128)S(1)}, f32[8192]{0:T(1024)S(1)}, f32[4,16,512]{2,1,0:T(8,128)}, ...), condition=%wide.region_4.6_spmd, body=%wide.region_2.5_spmd.sunk | while | flops 1111506432 | bytes 17993824 | solution.py:31
  170.0 23.8 %multiply_convert_fusion.6 = bf16[8192,512]{0,1:T(8,128)(2,1)S(1)} fusion(f32[16,8192]{1,0:T(8,128)S(1)} %get-tuple-element.416, f32[512]{0:T(512)S(1)} %fusion.69, f32[8192]{0:T(1024)S(1)} %get-tuple-element.414, f32[4,16,512]{2,1,0:T(8,128)} %get-tuple-element.415, s32[]{:T(128)S(6)} %copy.59), kind=kOutput, calls=%fused_computation.12.clone.1 | convolution fusion | flops 843055104 | bytes 8980484 | tf_op jit(solution)/shard_map/while/body/eval_jaxpr/dot_general | solution.py:11
  197.2 23.8 %multiply_convert_fusion.6 = bf16[8192,512]{0,1:T(8,128)(2,1)S(1)} fusion(f32[16,8192]{1,0:T(8,128)S(1)} %get-tuple-element.416, f32[512]{0:T(512)S(1)} %fusion.69, f32[8192]{0:T(1024)S(1)} %get-tuple-element.414, f32[4,16,512]{2,1,0:T(8,128)} %get-tuple-element.415, s32[]{:T(128)S(6)} %copy.59), kind=kOutput, calls=%fused_computation.12.clone.1 | convolution fusion | flops 843055104 | bytes 8980484 | tf_op jit(solution)/shard_map/while/body/eval_jaxpr/dot_general | solution.py:11
  224.4 23.8 %multiply_convert_fusion.6 = bf16[8192,512]{0,1:T(8,128)(2,1)S(1)} fusion(f32[16,8192]{1,0:T(8,128)S(1)} %get-tuple-element.416, f32[512]{0:T(512)S(1)} %fusion.69, f32[8192]{0:T(1024)S(1)} %get-tuple-element.414, f32[4,16,512]{2,1,0:T(8,128)} %get-tuple-element.415, s32[]{:T(128)S(6)} %copy.59), kind=kOutput, calls=%fused_computation.12.clone.1 | convolution fusion | flops 843055104 | bytes 8980484 | tf_op jit(solution)/shard_map/while/body/eval_jaxpr/dot_general | solution.py:11
  251.6 23.8 %multiply_convert_fusion.6 = bf16[8192,512]{0,1:T(8,128)(2,1)S(1)} fusion(f32[16,8192]{1,0:T(8,128)S(1)} %get-tuple-element.416, f32[512]{0:T(512)S(1)} %fusion.69, f32[8192]{0:T(1024)S(1)} %get-tuple-element.414, f32[4,16,512]{2,1,0:T(8,128)} %get-tuple-element.415, s32[]{:T(128)S(6)} %copy.59), kind=kOutput, calls=%fused_computation.12.clone.1 | convolution fusion | flops 843055104 | bytes 8980484 | tf_op jit(solution)/shard_map/while/body/eval_jaxpr/dot_general | solution.py:11
  294.7 131.7 %all-reduce.12.cloned.1.call-done = (f32[32,2048]{0,1:T(8,128)}, f32[4,16,512]{2,1,0:T(8,128)}) async-done(((f32[32,2048]{0,1:T(8,128)}, f32[4,16,512]{2,1,0:T(8,128)}), (f32[32,2048]{0,1:T(8,128)}, f32[4,16,512]{2,1,0:T(8,128)})) %all-reduce.12.cloned.1.call-update) | async-done | bytes 393232 | tf_op jit(solution)/shard_map/psum | solution.py:57
  450.4 102.8 %while.37 = (s32[]{:T(128)}, f32[4,32,512]{2,1,0:T(8,128)S(1)}, f32[8192]{0:T(1024)S(1)}, f32[4,16,512]{2,1,0:T(8,128)S(1)}, f32[16,8192]{1,0:T(8,128)S(1)}, /*index=5*/bf16[32,8192]{1,0:T(8,128)(2,1)S(1)}, s32[]{:T(128)}) while((s32[]{:T(128)}, f32[4,32,512]{2,1,0:T(8,128)S(1)}, f32[8192]{0:T(1024)S(1)}, f32[4,16,512]{2,1,0:T(8,128)S(1)}, ...), condition=%wide.region_10.13_spmd, body=%wide.region_8.12_spmd.sunk | while | flops 1111506432 | bytes 17993824 | solution.py:31
  450.4 23.0 %multiply_convert_fusion.7 = bf16[8192,512]{0,1:T(8,128)(2,1)S(1)} fusion(f32[16,8192]{1,0:T(8,128)S(1)} %get-tuple-element.437, f32[512]{0:T(512)S(1)} %fusion.75, f32[8192]{0:T(1024)S(1)} %get-tuple-element.435, f32[4,16,512]{2,1,0:T(8,128)S(1)} %get-tuple-element.436, s32[]{:T(128)S(6)} %copy.67), kind=kOutput, calls=%fused_computation.24.clone.1 | convolution fusion | flops 843055104 | bytes 8980484 | tf_op jit(solution)/shard_map/while/body/eval_jaxpr/dot_general | solution.py:11
  476.1 23.1 %multiply_convert_fusion.7 = bf16[8192,512]{0,1:T(8,128)(2,1)S(1)} fusion(f32[16,8192]{1,0:T(8,128)S(1)} %get-tuple-element.437, f32[512]{0:T(512)S(1)} %fusion.75, f32[8192]{0:T(1024)S(1)} %get-tuple-element.435, f32[4,16,512]{2,1,0:T(8,128)S(1)} %get-tuple-element.436, s32[]{:T(128)S(6)} %copy.67), kind=kOutput, calls=%fused_computation.24.clone.1 | convolution fusion | flops 843055104 | bytes 8980484 | tf_op jit(solution)/shard_map/while/body/eval_jaxpr/dot_general | solution.py:11
  501.8 23.1 %multiply_convert_fusion.7 = bf16[8192,512]{0,1:T(8,128)(2,1)S(1)} fusion(f32[16,8192]{1,0:T(8,128)S(1)} %get-tuple-element.437, f32[512]{0:T(512)S(1)} %fusion.75, f32[8192]{0:T(1024)S(1)} %get-tuple-element.435, f32[4,16,512]{2,1,0:T(8,128)S(1)} %get-tuple-element.436, s32[]{:T(128)S(6)} %copy.67), kind=kOutput, calls=%fused_computation.24.clone.1 | convolution fusion | flops 843055104 | bytes 8980484 | tf_op jit(solution)/shard_map/while/body/eval_jaxpr/dot_general | solution.py:11
  527.5 23.1 %multiply_convert_fusion.7 = bf16[8192,512]{0,1:T(8,128)(2,1)S(1)} fusion(f32[16,8192]{1,0:T(8,128)S(1)} %get-tuple-element.437, f32[512]{0:T(512)S(1)} %fusion.75, f32[8192]{0:T(1024)S(1)} %get-tuple-element.435, f32[4,16,512]{2,1,0:T(8,128)S(1)} %get-tuple-element.436, s32[]{:T(128)S(6)} %copy.67), kind=kOutput, calls=%fused_computation.24.clone.1 | convolution fusion | flops 843055104 | bytes 8980484 | tf_op jit(solution)/shard_map/while/body/eval_jaxpr/dot_general | solution.py:11
  576.3 138.1 %all-reduce.8.cloned.1.call-done = f32[32,2048]{0,1:T(8,128)} async-done(((f32[32,2048]{0,1:T(8,128)}), f32[32,2048]{0,1:T(8,128)}) %all-reduce.8.cloned.1.call-update) | async-done | bytes 262160 | tf_op jit(solution)/shard_map/psum | solution.py:57
  741.1 210.8 %while.38 = (s32[]{:T(128)}, f32[8,32,512]{2,1,0:T(8,128)}, f32[8192]{0:T(1024)S(1)}, f32[8,16,512]{2,0,1:T(8,128)S(1)}, f32[16,8192]{1,0:T(8,128)S(1)}, /*index=5*/bf16[32,8192]{1,0:T(8,128)(2,1)S(1)}, s32[]{:T(128)}) while((s32[]{:T(128)}, f32[8,32,512]{2,1,0:T(8,128)}, f32[8192]{0:T(1024)S(1)}, f32[8,16,512]{2,0,1:T(8,128)S(1)}, ...), condition=%wide.region_15.18_spmd, body=%wide.region_13.17_spmd.sunk | while | flops 1111506432 | bytes 18059356 | solution.py:31
  741.2 23.0 %multiply_convert_fusion.8 = bf16[8192,512]{0,1:T(8,128)(2,1)S(1)} fusion(f32[16,8192]{1,0:T(8,128)S(1)} %get-tuple-element.458, f32[512]{0:T(512)S(1)} %multiply_reduce_fusion.3, f32[8192]{0:T(1024)S(1)} %get-tuple-element.456, f32[1,16,512]{2,0,1:T(1,128)S(1)} %constant_dynamic-slice_fusion.2), kind=kOutput, calls=%fused_computation.36.clone.1 | convolution fusion | flops 843055104 | bytes 8980480 | tf_op jit(solution)/shard_map/while/body/eval_jaxpr/dot_general | solution.py:11
  767.5 23.0 %multiply_convert_fusion.8 = bf16[8192,512]{0,1:T(8,128)(2,1)S(1)} fusion(f32[16,8192]{1,0:T(8,128)S(1)} %get-tuple-element.458, f32[512]{0:T(512)S(1)} %multiply_reduce_fusion.3, f32[8192]{0:T(1024)S(1)} %get-tuple-element.456, f32[1,16,512]{2,0,1:T(1,128)S(1)} %constant_dynamic-slice_fusion.2), kind=kOutput, calls=%fused_computation.36.clone.1 | convolution fusion | flops 843055104 | bytes 8980480 | tf_op jit(solution)/shard_map/while/body/eval_jaxpr/dot_general | solution.py:11
  793.9 23.0 %multiply_convert_fusion.8 = bf16[8192,512]{0,1:T(8,128)(2,1)S(1)} fusion(f32[16,8192]{1,0:T(8,128)S(1)} %get-tuple-element.458, f32[512]{0:T(512)S(1)} %multiply_reduce_fusion.3, f32[8192]{0:T(1024)S(1)} %get-tuple-element.456, f32[1,16,512]{2,0,1:T(1,128)S(1)} %constant_dynamic-slice_fusion.2), kind=kOutput, calls=%fused_computation.36.clone.1 | convolution fusion | flops 843055104 | bytes 8980480 | tf_op jit(solution)/shard_map/while/body/eval_jaxpr/dot_general | solution.py:11
  820.2 23.0 %multiply_convert_fusion.8 = bf16[8192,512]{0,1:T(8,128)(2,1)S(1)} fusion(f32[16,8192]{1,0:T(8,128)S(1)} %get-tuple-element.458, f32[512]{0:T(512)S(1)} %multiply_reduce_fusion.3, f32[8192]{0:T(1024)S(1)} %get-tuple-element.456, f32[1,16,512]{2,0,1:T(1,128)S(1)} %constant_dynamic-slice_fusion.2), kind=kOutput, calls=%fused_computation.36.clone.1 | convolution fusion | flops 843055104 | bytes 8980480 | tf_op jit(solution)/shard_map/while/body/eval_jaxpr/dot_general | solution.py:11
  846.6 23.0 %multiply_convert_fusion.8 = bf16[8192,512]{0,1:T(8,128)(2,1)S(1)} fusion(f32[16,8192]{1,0:T(8,128)S(1)} %get-tuple-element.458, f32[512]{0:T(512)S(1)} %multiply_reduce_fusion.3, f32[8192]{0:T(1024)S(1)} %get-tuple-element.456, f32[1,16,512]{2,0,1:T(1,128)S(1)} %constant_dynamic-slice_fusion.2), kind=kOutput, calls=%fused_computation.36.clone.1 | convolution fusion | flops 843055104 | bytes 8980480 | tf_op jit(solution)/shard_map/while/body/eval_jaxpr/dot_general | solution.py:11
  872.9 23.0 %multiply_convert_fusion.8 = bf16[8192,512]{0,1:T(8,128)(2,1)S(1)} fusion(f32[16,8192]{1,0:T(8,128)S(1)} %get-tuple-element.458, f32[512]{0:T(512)S(1)} %multiply_reduce_fusion.3, f32[8192]{0:T(1024)S(1)} %get-tuple-element.456, f32[1,16,512]{2,0,1:T(1,128)S(1)} %constant_dynamic-slice_fusion.2), kind=kOutput, calls=%fused_computation.36.clone.1 | convolution fusion | flops 843055104 | bytes 8980480 | tf_op jit(solution)/shard_map/while/body/eval_jaxpr/dot_general | solution.py:11
  899.3 23.0 %multiply_convert_fusion.8 = bf16[8192,512]{0,1:T(8,128)(2,1)S(1)} fusion(f32[16,8192]{1,0:T(8,128)S(1)} %get-tuple-element.458, f32[512]{0:T(512)S(1)} %multiply_reduce_fusion.3, f32[8192]{0:T(1024)S(1)} %get-tuple-element.456, f32[1,16,512]{2,0,1:T(1,128)S(1)} %constant_dynamic-slice_fusion.2), kind=kOutput, calls=%fused_computation.36.clone.1 | convolution fusion | flops 843055104 | bytes 8980480 | tf_op jit(solution)/shard_map/while/body/eval_jaxpr/dot_general | solution.py:11
  925.6 23.0 %multiply_convert_fusion.8 = bf16[8192,512]{0,1:T(8,128)(2,1)S(1)} fusion(f32[16,8192]{1,0:T(8,128)S(1)} %get-tuple-element.458, f32[512]{0:T(512)S(1)} %multiply_reduce_fusion.3, f32[8192]{0:T(1024)S(1)} %get-tuple-element.456, f32[1,16,512]{2,0,1:T(1,128)S(1)} %constant_dynamic-slice_fusion.2), kind=kOutput, calls=%fused_computation.36.clone.1 | convolution fusion | flops 843055104 | bytes 8980480 | tf_op jit(solution)/shard_map/while/body/eval_jaxpr/dot_general | solution.py:11
  953.8 21.0 %reduce-scatter.2.cloned.1.call-done = f32[32,1024]{1,0:T(8,128)} async-done(((f32[32,4096]{1,0:T(8,128)}), f32[32,1024]{1,0:T(8,128)}) %reduce-scatter.2.cloned.1.call-update) | async-done | bytes 131088 | tf_op jit(solution)/shard_map/reduce_scatter | solution.py:65
  982.0 97.5 %all-reduce.10.cloned.1.call-done = f32[32,1024]{1,0:T(8,128)} async-done(((f32[32,1024]{1,0:T(8,128)}), f32[32,1024]{1,0:T(8,128)}) %all-reduce.10.cloned.1.call-update) | async-done | bytes 131088 | tf_op jit(solution)/shard_map/psum | solution.py:66
  (111 shorter events, 208.7 us)
Async XLA Ops:
  7.2 30.1 %copy-start.1 = (f32[16,8192]{1,0:T(8,128)S(1)}, f32[16,8192]{1,0:T(8,128)}, u32[]{:S(2)}) copy-start(f32[16,8192]{1,0:T(8,128)} %param.16) | copy-start | bytes 1572868
  7.2 30.2 %copy-start = (f32[32,8192]{1,0:T(8,128)S(1)}, f32[32,8192]{1,0:T(8,128)}, u32[]{:S(2)}) copy-start(f32[32,8192]{1,0:T(8,128)} %param.17) | copy-start | bytes 3145732
  7.2 161.9 %all-reduce.6.cloned.1.call-start = ((), (), s32[]{:S(2)}) async-start(), calls=%async_computation.1 | async-start | bytes 262144 | tf_op jit(solution)/shard_map/psum | solution.py:52
  8.1 29.2 %copy-start.5 = (f32[1,2048]{1,0:T(1,128)}, f32[1,2048]{1,0:T(1,128)S(1)}, u32[]{:S(2)}) copy-start(f32[1,2048]{1,0:T(1,128)S(1)} %get-tuple-element.283) | copy-start | bytes 24580
  25.6 400.7 %all-reduce.12.cloned.1.call-start = ((), (), s32[]{:S(2)}) async-start(), calls=%async_computation.5 | async-start | bytes 2359296 | tf_op jit(solution)/shard_map/psum | solution.py:57
  25.7 27.9 %copy-start.8 = (pred[2048]{0:T(1024)(128)(4,1)}, pred[2048]{0:T(1024)(128)(4,1)S(1)}, u32[]{:S(2)}) copy-start(pred[2048]{0:T(1024)(128)(4,1)S(1)} %compare_and_fusion) | copy-start | bytes 6148
  169.1 109.3 %copy-start.3 = (f32[2048,32]{1,0:T(8,128)S(1)}, f32[2048,32]{1,0:T(8,128)}, u32[]{:S(2)}) copy-start(f32[2048,32]{1,0:T(8,128)} %gather_fusion.2) | copy-start | bytes 786436
  281.0 433.3 %all-reduce.8.cloned.1.call-start = ((), (), s32[]{:S(2)}) async-start(), calls=%async_computation.2 | async-start | bytes 2097152 | tf_op jit(solution)/shard_map/psum | solution.py:57
  442.1 8.3 copy-start.4
  450.4 113.0 %copy-start.2 = (f32[2048,32]{1,0:T(8,128)S(1)}, f32[2048,32]{1,0:T(8,128)}, u32[]{:S(2)}) copy-start(f32[2048,32]{1,0:T(8,128)} %gather_fusion.5) | copy-start | bytes 786436
  450.4 113.0 %copy-start.6 = (f32[1,2048]{1,0:T(1,128)S(1)}, f32[1,2048]{1,0:T(1,128)}, u32[]{:S(2)}) copy-start(f32[1,2048]{1,0:T(1,128)} %copy-done.5) | copy-start | bytes 24580
  450.4 113.0 %copy-start.9 = (pred[2048]{0:T(1024)(128)(4,1)S(1)}, pred[2048]{0:T(1024)(128)(4,1)}, u32[]{:S(2)}) copy-start(pred[2048]{0:T(1024)(128)(4,1)} %copy-done.8) | copy-start | bytes 6148
  553.2 12.9 %copy-start.7 = (f32[16,1024]{1,0:T(8,128)S(1)}, f32[16,1024]{1,0:T(8,128)}, u32[]{:S(2)}) copy-start(f32[16,1024]{1,0:T(8,128)} %param.21) | copy-start | bytes 196612
  566.0 408.8 %reduce-scatter.2.cloned.1.call-start = ((), (), s32[]{:S(2)}) async-start(), calls=%async_computation.3 | async-start | bytes 655360 | tf_op jit(solution)/shard_map/reduce_scatter | solution.py:65
  953.8 125.7 %all-reduce.10.cloned.1.call-start = ((), (), s32[]{:S(2)}) async-start(), calls=%async_computation.4 | async-start | bytes 262144 | tf_op jit(solution)/shard_map/psum | solution.py:66
Sparse Core Ops, SparseCore 0:
  25.7 143.2 all-reduce.5
  281.2 145.1 all-reduce.11
  566.1 148.1 all-reduce.7
  953.9 20.8 reduce-scatter.1
  978.2 101.2 all-reduce.9
where the time goes:
time: 1100 us; the launch traced here: 1090 us
  waiting for transfers between devices  493 us (45%)
  matrix products  419 us (38%)
  local copies, waits for them, and re-layouts  87.6 us (8%)
  other arithmetic  63.8 us (6%)
  between operations  14.4 us (1%)
    dot_general x16, matrix products, matern_tile(): jnp.dot(points_block.T, queries, precision=lax.Precision.HIGHEST, preferr...  372 us
    psum x2, waiting for transfers between devices, per_device(): gradient = lax.psum(partial_sums + own_terms, ('rows', 'cols'))  270 us
    psum x1, waiting for transfers between devices, per_device(): lax.psum(take_owned(points, safe_rows, weights), ('rows', 'cols'))  105 us
    psum x1, waiting for transfers between devices, per_device(): slab_sum = lax.psum(slab_sum, 'rows')  97.5 us
    gather x6, local copies, waits for them, and re-layouts, take_owned(): return jnp.take(array, safe_rows, axis=1) * weights[None, :]  58.9 us
    dot_general x16, matrix products, apply_block(): jnp.dot(coeff_half, matern_tile(points, block), preferred_element_type=jn...  46.8 us
    scatter-add x2, other arithmetic, per_device(): jnp.zeros_like(coeffs_now).at[:, safe_rows].add(gradient * weights[None, :])  31.4 us
    unnamed x28, local copies, waits for them, and re-layouts  22.4 us
  transfers between devices with their start and end apart: 5, of which 5 were waited for; matrix products, arithmetic and copies ran while one was open for 5% of the time, Pallas kernels for 0%

commit v1 on v0

--- a/solution.py
+++ b/solution.py
@@ -63,7 +63,11 @@
         points, coeff_half, lax.all_gather(test_points, "cols", axis=1, tiled=True)
     )
     slab_sum = lax.psum_scatter(partial_test, "cols", scatter_dimension=1, tiled=True)
-    slab_sum = lax.psum(slab_sum, "rows")
+    n_dev, total = (lax.axis_size("rows"), slab_sum)
+    for reach in [1 << k for k in range(n_dev.bit_length() - 1)]:
+        swap = [(i, i ^ reach) for i in range(n_dev)]
+        total = total + lax.ppermute(total, "rows", swap)
+    slab_sum = total
     return (coeffs_now, velocity_now, slab_sum)
 
 

time: 1100 us -> 1020 us (0.927)
  waiting for transfers between devices: 493 us -> 405 us
    psum x1 -> x0, waiting for transfers between devices: 97.5 us -> none  [per_device(): slab_sum = lax.psum(slab_sum, 'rows')]
    unnamed x28 -> x27, local copies, waits for them, and re-layouts: 22.4 us -> 20.8 us
  transfers between devices with their start and end apart: 5 -> 9, of which waited for: 5 -> 8; matrix products, arithmetic and copies ran while one was open for 5% -> 6% of each run, Pallas kernels for 0% -> 0%
where the time goes in v1:
time: 1020 us; the launch traced here: 1010 us
  matrix products  419 us (41%)
  waiting for transfers between devices  405 us (40%)
  local copies, waits for them, and re-layouts  86.1 us (8%)
  other arithmetic  65.5 us (6%)
  between operations  14.4 us (1%)
  starting transfers between devices  11.2 us (1%)
    dot_general x16, matrix products, matern_tile(): jnp.dot(points_block.T, queries, precision=lax.Precision.HIGHEST, preferr...  372 us
    psum x2, waiting for transfers between devices, per_device(): gradient = lax.psum(partial_sums + own_terms, ('rows', 'cols'))  270 us
    psum x1, waiting for transfers between devices, per_device(): lax.psum(take_owned(points, safe_rows, weights), ('rows', 'cols'))  105 us
    gather x6, local copies, waits for them, and re-layouts, take_owned(): return jnp.take(array, safe_rows, axis=1) * weights[None, :]  58.9 us
    dot_general x16, matrix products, apply_block(): jnp.dot(coeff_half, matern_tile(points, block), preferred_element_type=jn...  46.8 us
    scatter-add x2, other arithmetic, per_device(): jnp.zeros_like(coeffs_now).at[:, safe_rows].add(gradient * weights[None, :])  31.4 us
    reduce_scatter x1, waiting for transfers between devices, per_device(): lax.psum_scatter(partial_test, 'cols', scatter_dimension=1, tiled=True)  21 us
    unnamed x27, local copies, waits for them, and re-layouts  20.8 us
  transfers between devices with their start and end apart: 9, of which 8 were waited for; matrix products, arithmetic and copies ran while one was open for 6% of the time, Pallas kernels for 0%

profile of v1, /device:TPU:1, one launch (start us, length us, event | category | flops | bytes accessed | tf_op | source)
XLA Modules:
  0.0 1011.1 jit_solution(12448964507558421555)
XLA Ops:
  64.4 104.7 %all-reduce.5.cloned.1.call-done = f32[4,16,512]{2,1,0:T(8,128)} async-done(((f32[4,16,512]{2,1,0:T(8,128)}), f32[4,16,512]{2,1,0:T(8,128)}) %all-reduce.5.cloned.1.call-update) | async-done | bytes 131088 | tf_op jit(solution)/shard_map/psum | solution.py:52
  169.1 109.0 %while.36 = (s32[]{:T(128)}, f32[4,32,512]{2,1,0:T(8,128)S(1)}, f32[8192]{0:T(1024)S(1)}, f32[4,16,512]{2,1,0:T(8,128)}, f32[16,8192]{1,0:T(8,128)S(1)}, /*index=5*/bf16[32,8192]{1,0:T(8,128)(2,1)S(1)}, s32[]{:T(128)}) while((s32[]{:T(128)}, f32[4,32,512]{2,1,0:T(8,128)S(1)}, f32[8192]{0:T(1024)S(1)}, f32[4,16,512]{2,1,0:T(8,128)}, ...), condition=%wide.region_4.6_spmd, body=%wide.region_2.5_spmd.sunk | while | flops 1111506432 | bytes 17993824 | solution.py:31
  170.0 23.8 %multiply_convert_fusion.6 = bf16[8192,512]{0,1:T(8,128)(2,1)S(1)} fusion(f32[16,8192]{1,0:T(8,128)S(1)} %get-tuple-element.416, f32[512]{0:T(512)S(1)} %fusion.69, f32[8192]{0:T(1024)S(1)} %get-tuple-element.414, f32[4,16,512]{2,1,0:T(8,128)} %get-tuple-element.415, s32[]{:T(128)S(6)} %copy.59), kind=kOutput, calls=%fused_computation.12.clone.1 | convolution fusion | flops 843055104 | bytes 8980484 | tf_op jit(solution)/shard_map/while/body/eval_jaxpr/dot_general | solution.py:11
  197.2 23.8 %multiply_convert_fusion.6 = bf16[8192,512]{0,1:T(8,128)(2,1)S(1)} fusion(f32[16,8192]{1,0:T(8,128)S(1)} %get-tuple-element.416, f32[512]{0:T(512)S(1)} %fusion.69, f32[8192]{0:T(1024)S(1)} %get-tuple-element.414, f32[4,16,512]{2,1,0:T(8,128)} %get-tuple-element.415, s32[]{:T(128)S(6)} %copy.59), kind=kOutput, calls=%fused_computation.12.clone.1 | convolution fusion | flops 843055104 | bytes 8980484 | tf_op jit(solution)/shard_map/while/body/eval_jaxpr/dot_general | solution.py:11
  224.4 23.8 %multiply_convert_fusion.6 = bf16[8192,512]{0,1:T(8,128)(2,1)S(1)} fusion(f32[16,8192]{1,0:T(8,128)S(1)} %get-tuple-element.416, f32[512]{0:T(512)S(1)} %fusion.69, f32[8192]{0:T(1024)S(1)} %get-tuple-element.414, f32[4,16,512]{2,1,0:T(8,128)} %get-tuple-element.415, s32[]{:T(128)S(6)} %copy.59), kind=kOutput, calls=%fused_computation.12.clone.1 | convolution fusion | flops 843055104 | bytes 8980484 | tf_op jit(solution)/shard_map/while/body/eval_jaxpr/dot_general | solution.py:11
  251.7 23.8 %multiply_convert_fusion.6 = bf16[8192,512]{0,1:T(8,128)(2,1)S(1)} fusion(f32[16,8192]{1,0:T(8,128)S(1)} %get-tuple-element.416, f32[512]{0:T(512)S(1)} %fusion.69, f32[8192]{0:T(1024)S(1)} %get-tuple-element.414, f32[4,16,512]{2,1,0:T(8,128)} %get-tuple-element.415, s32[]{:T(128)S(6)} %copy.59), kind=kOutput, calls=%fused_computation.12.clone.1 | convolution fusion | flops 843055104 | bytes 8980484 | tf_op jit(solution)/shard_map/while/body/eval_jaxpr/dot_general | solution.py:11
  294.7 131.7 %all-reduce.9.cloned.1.call-done = (f32[32,2048]{0,1:T(8,128)}, f32[4,16,512]{2,1,0:T(8,128)}) async-done(((f32[32,2048]{0,1:T(8,128)}, f32[4,16,512]{2,1,0:T(8,128)}), (f32[32,2048]{0,1:T(8,128)}, f32[4,16,512]{2,1,0:T(8,128)})) %all-reduce.9.cloned.1.call-update) | async-done | bytes 393232 | tf_op jit(solution)/shard_map/psum | solution.py:57
  426.4 15.7 %scatter_custom_fusion = f32[32,8192]{0,1:T(8,128)} fusion(s32[2048]{0:T(1024)S(1)} %bitcast.194, f32[]{:T(128)} %constant.138.clone.1, f32[32,2048]{0,1:T(8,128)} %get-tuple-element.272, f32[2048]{0:T(1024)S(1)} %bitcast.188), kind=kCustom, calls=%fused_computation.46 | custom fusion | flops 131072 | bytes 1318916 | tf_op jit(solution)/shard_map/scatter-add | solution.py:58
  450.4 102.8 %while.37 = (s32[]{:T(128)}, f32[4,32,512]{2,1,0:T(8,128)S(1)}, f32[8192]{0:T(1024)S(1)}, f32[4,16,512]{2,1,0:T(8,128)S(1)}, f32[16,8192]{1,0:T(8,128)S(1)}, /*index=5*/bf16[32,8192]{1,0:T(8,128)(2,1)S(1)}, s32[]{:T(128)}) while((s32[]{:T(128)}, f32[4,32,512]{2,1,0:T(8,128)S(1)}, f32[8192]{0:T(1024)S(1)}, f32[4,16,512]{2,1,0:T(8,128)S(1)}, ...), condition=%wide.region_10.13_spmd, body=%wide.region_8.12_spmd.sunk | while | flops 1111506432 | bytes 17993824 | solution.py:31
  450.5 23.1 %multiply_convert_fusion.7 = bf16[8192,512]{0,1:T(8,128)(2,1)S(1)} fusion(f32[16,8192]{1,0:T(8,128)S(1)} %get-tuple-element.437, f32[512]{0:T(512)S(1)} %fusion.75, f32[8192]{0:T(1024)S(1)} %get-tuple-element.435, f32[4,16,512]{2,1,0:T(8,128)S(1)} %get-tuple-element.436, s32[]{:T(128)S(6)} %copy.67), kind=kOutput, calls=%fused_computation.24.clone.1 | convolution fusion | flops 843055104 | bytes 8980484 | tf_op jit(solution)/shard_map/while/body/eval_jaxpr/dot_general | solution.py:11
  476.2 23.1 %multiply_convert_fusion.7 = bf16[8192,512]{0,1:T(8,128)(2,1)S(1)} fusion(f32[16,8192]{1,0:T(8,128)S(1)} %get-tuple-element.437, f32[512]{0:T(512)S(1)} %fusion.75, f32[8192]{0:T(1024)S(1)} %get-tuple-element.435, f32[4,16,512]{2,1,0:T(8,128)S(1)} %get-tuple-element.436, s32[]{:T(128)S(6)} %copy.67), kind=kOutput, calls=%fused_computation.24.clone.1 | convolution fusion | flops 843055104 | bytes 8980484 | tf_op jit(solution)/shard_map/while/body/eval_jaxpr/dot_general | solution.py:11
  501.9 23.1 %multiply_convert_fusion.7 = bf16[8192,512]{0,1:T(8,128)(2,1)S(1)} fusion(f32[16,8192]{1,0:T(8,128)S(1)} %get-tuple-element.437, f32[512]{0:T(512)S(1)} %fusion.75, f32[8192]{0:T(1024)S(1)} %get-tuple-element.435, f32[4,16,512]{2,1,0:T(8,128)S(1)} %get-tuple-element.436, s32[]{:T(128)S(6)} %copy.67), kind=kOutput, calls=%fused_computation.24.clone.1 | convolution fusion | flops 843055104 | bytes 8980484 | tf_op jit(solution)/shard_map/while/body/eval_jaxpr/dot_general | solution.py:11
  527.6 23.1 %multiply_convert_fusion.7 = bf16[8192,512]{0,1:T(8,128)(2,1)S(1)} fusion(f32[16,8192]{1,0:T(8,128)S(1)} %get-tuple-element.437, f32[512]{0:T(512)S(1)} %fusion.75, f32[8192]{0:T(1024)S(1)} %get-tuple-element.435, f32[4,16,512]{2,1,0:T(8,128)S(1)} %get-tuple-element.436, s32[]{:T(128)S(6)} %copy.67), kind=kOutput, calls=%fused_computation.24.clone.1 | convolution fusion | flops 843055104 | bytes 8980484 | tf_op jit(solution)/shard_map/while/body/eval_jaxpr/dot_general | solution.py:11
  576.3 138.1 %all-reduce.7.cloned.1.call-done = f32[32,2048]{0,1:T(8,128)} async-done(((f32[32,2048]{0,1:T(8,128)}), f32[32,2048]{0,1:T(8,128)}) %all-reduce.7.cloned.1.call-update) | async-done | bytes 262160 | tf_op jit(solution)/shard_map/psum | solution.py:57
  741.2 210.8 %while.38 = (s32[]{:T(128)}, f32[8,32,512]{2,1,0:T(8,128)}, f32[8192]{0:T(1024)S(1)}, f32[8,16,512]{2,0,1:T(8,128)S(1)}, f32[16,8192]{1,0:T(8,128)S(1)}, /*index=5*/bf16[32,8192]{1,0:T(8,128)(2,1)S(1)}, s32[]{:T(128)}) while((s32[]{:T(128)}, f32[8,32,512]{2,1,0:T(8,128)}, f32[8192]{0:T(1024)S(1)}, f32[8,16,512]{2,0,1:T(8,128)S(1)}, ...), condition=%wide.region_15.18_spmd, body=%wide.region_13.17_spmd.sunk | while | flops 1111506432 | bytes 18059356 | solution.py:31
  741.3 23.0 %multiply_convert_fusion.8 = bf16[8192,512]{0,1:T(8,128)(2,1)S(1)} fusion(f32[16,8192]{1,0:T(8,128)S(1)} %get-tuple-element.458, f32[512]{0:T(512)S(1)} %multiply_reduce_fusion.3, f32[8192]{0:T(1024)S(1)} %get-tuple-element.456, f32[1,16,512]{2,0,1:T(1,128)S(1)} %constant_dynamic-slice_fusion.2), kind=kOutput, calls=%fused_computation.36.clone.1 | convolution fusion | flops 843055104 | bytes 8980480 | tf_op jit(solution)/shard_map/while/body/eval_jaxpr/dot_general | solution.py:11
  767.6 23.0 %multiply_convert_fusion.8 = bf16[8192,512]{0,1:T(8,128)(2,1)S(1)} fusion(f32[16,8192]{1,0:T(8,128)S(1)} %get-tuple-element.458, f32[512]{0:T(512)S(1)} %multiply_reduce_fusion.3, f32[8192]{0:T(1024)S(1)} %get-tuple-element.456, f32[1,16,512]{2,0,1:T(1,128)S(1)} %constant_dynamic-slice_fusion.2), kind=kOutput, calls=%fused_computation.36.clone.1 | convolution fusion | flops 843055104 | bytes 8980480 | tf_op jit(solution)/shard_map/while/body/eval_jaxpr/dot_general | solution.py:11
  793.9 23.0 %multiply_convert_fusion.8 = bf16[8192,512]{0,1:T(8,128)(2,1)S(1)} fusion(f32[16,8192]{1,0:T(8,128)S(1)} %get-tuple-element.458, f32[512]{0:T(512)S(1)} %multiply_reduce_fusion.3, f32[8192]{0:T(1024)S(1)} %get-tuple-element.456, f32[1,16,512]{2,0,1:T(1,128)S(1)} %constant_dynamic-slice_fusion.2), kind=kOutput, calls=%fused_computation.36.clone.1 | convolution fusion | flops 843055104 | bytes 8980480 | tf_op jit(solution)/shard_map/while/body/eval_jaxpr/dot_general | solution.py:11
  820.3 23.0 %multiply_convert_fusion.8 = bf16[8192,512]{0,1:T(8,128)(2,1)S(1)} fusion(f32[16,8192]{1,0:T(8,128)S(1)} %get-tuple-element.458, f32[512]{0:T(512)S(1)} %multiply_reduce_fusion.3, f32[8192]{0:T(1024)S(1)} %get-tuple-element.456, f32[1,16,512]{2,0,1:T(1,128)S(1)} %constant_dynamic-slice_fusion.2), kind=kOutput, calls=%fused_computation.36.clone.1 | convolution fusion | flops 843055104 | bytes 8980480 | tf_op jit(solution)/shard_map/while/body/eval_jaxpr/dot_general | solution.py:11
  846.6 23.0 %multiply_convert_fusion.8 = bf16[8192,512]{0,1:T(8,128)(2,1)S(1)} fusion(f32[16,8192]{1,0:T(8,128)S(1)} %get-tuple-element.458, f32[512]{0:T(512)S(1)} %multiply_reduce_fusion.3, f32[8192]{0:T(1024)S(1)} %get-tuple-element.456, f32[1,16,512]{2,0,1:T(1,128)S(1)} %constant_dynamic-slice_fusion.2), kind=kOutput, calls=%fused_computation.36.clone.1 | convolution fusion | flops 843055104 | bytes 8980480 | tf_op jit(solution)/shard_map/while/body/eval_jaxpr/dot_general | solution.py:11
  873.0 23.0 %multiply_convert_fusion.8 = bf16[8192,512]{0,1:T(8,128)(2,1)S(1)} fusion(f32[16,8192]{1,0:T(8,128)S(1)} %get-tuple-element.458, f32[512]{0:T(512)S(1)} %multiply_reduce_fusion.3, f32[8192]{0:T(1024)S(1)} %get-tuple-element.456, f32[1,16,512]{2,0,1:T(1,128)S(1)} %constant_dynamic-slice_fusion.2), kind=kOutput, calls=%fused_computation.36.clone.1 | convolution fusion | flops 843055104 | bytes 8980480 | tf_op jit(solution)/shard_map/while/body/eval_jaxpr/dot_general | solution.py:11
  899.3 23.0 %multiply_convert_fusion.8 = bf16[8192,512]{0,1:T(8,128)(2,1)S(1)} fusion(f32[16,8192]{1,0:T(8,128)S(1)} %get-tuple-element.458, f32[512]{0:T(512)S(1)} %multiply_reduce_fusion.3, f32[8192]{0:T(1024)S(1)} %get-tuple-element.456, f32[1,16,512]{2,0,1:T(1,128)S(1)} %constant_dynamic-slice_fusion.2), kind=kOutput, calls=%fused_computation.36.clone.1 | convolution fusion | flops 843055104 | bytes 8980480 | tf_op jit(solution)/shard_map/while/body/eval_jaxpr/dot_general | solution.py:11
  925.6 23.0 %multiply_convert_fusion.8 = bf16[8192,512]{0,1:T(8,128)(2,1)S(1)} fusion(f32[16,8192]{1,0:T(8,128)S(1)} %get-tuple-element.458, f32[512]{0:T(512)S(1)} %multiply_reduce_fusion.3, f32[8192]{0:T(1024)S(1)} %get-tuple-element.456, f32[1,16,512]{2,0,1:T(1,128)S(1)} %constant_dynamic-slice_fusion.2), kind=kOutput, calls=%fused_computation.36.clone.1 | convolution fusion | flops 843055104 | bytes 8980480 | tf_op jit(solution)/shard_map/while/body/eval_jaxpr/dot_general | solution.py:11
  953.8 21.0 %reduce-scatter.2.cloned.1.call-done = f32[32,1024]{1,0:T(8,128)} async-done(((f32[32,4096]{1,0:T(8,128)}), f32[32,1024]{1,0:T(8,128)}) %reduce-scatter.2.cloned.1.call-update) | async-done | bytes 131088 | tf_op jit(solution)/shard_map/reduce_scatter | solution.py:65
  (122 shorter events, 213.5 us)
Async XLA Ops:
  7.2 30.1 %copy-start.1 = (f32[16,8192]{1,0:T(8,128)S(1)}, f32[16,8192]{1,0:T(8,128)}, u32[]{:S(2)}) copy-start(f32[16,8192]{1,0:T(8,128)} %param.16) | copy-start | bytes 1572868
  7.2 30.2 %copy-start = (f32[32,8192]{1,0:T(8,128)S(1)}, f32[32,8192]{1,0:T(8,128)}, u32[]{:S(2)}) copy-start(f32[32,8192]{1,0:T(8,128)} %param.17) | copy-start | bytes 3145732
  7.2 161.9 %all-reduce.5.cloned.1.call-start = ((), (), s32[]{:S(2)}) async-start(), calls=%async_computation.1 | async-start | bytes 262144 | tf_op jit(solution)/shard_map/psum | solution.py:52
  8.1 29.2 %copy-start.5 = (f32[1,2048]{1,0:T(1,128)}, f32[1,2048]{1,0:T(1,128)S(1)}, u32[]{:S(2)}) copy-start(f32[1,2048]{1,0:T(1,128)S(1)} %get-tuple-element.283) | copy-start | bytes 24580
  25.6 400.8 %all-reduce.9.cloned.1.call-start = ((), (), s32[]{:S(2)}) async-start(), calls=%async_computation.4 | async-start | bytes 2359296 | tf_op jit(solution)/shard_map/psum | solution.py:57
  25.7 27.9 %copy-start.8 = (pred[2048]{0:T(1024)(128)(4,1)}, pred[2048]{0:T(1024)(128)(4,1)S(1)}, u32[]{:S(2)}) copy-start(pred[2048]{0:T(1024)(128)(4,1)S(1)} %compare_and_fusion) | copy-start | bytes 6148
  169.1 109.3 %copy-start.3 = (f32[2048,32]{1,0:T(8,128)S(1)}, f32[2048,32]{1,0:T(8,128)}, u32[]{:S(2)}) copy-start(f32[2048,32]{1,0:T(8,128)} %gather_fusion.2) | copy-start | bytes 786436
  281.1 433.3 %all-reduce.7.cloned.1.call-start = ((), (), s32[]{:S(2)}) async-start(), calls=%async_computation.2 | async-start | bytes 2097152 | tf_op jit(solution)/shard_map/psum | solution.py:57
  442.1 8.3 copy-start.4
  450.4 113.0 %copy-start.2 = (f32[2048,32]{1,0:T(8,128)S(1)}, f32[2048,32]{1,0:T(8,128)}, u32[]{:S(2)}) copy-start(f32[2048,32]{1,0:T(8,128)} %gather_fusion.5) | copy-start | bytes 786436
  450.4 113.0 %copy-start.6 = (f32[1,2048]{1,0:T(1,128)S(1)}, f32[1,2048]{1,0:T(1,128)}, u32[]{:S(2)}) copy-start(f32[1,2048]{1,0:T(1,128)} %copy-done.5) | copy-start | bytes 24580
  450.4 113.0 %copy-start.9 = (pred[2048]{0:T(1024)(128)(4,1)S(1)}, pred[2048]{0:T(1024)(128)(4,1)}, u32[]{:S(2)}) copy-start(pred[2048]{0:T(1024)(128)(4,1)} %copy-done.8) | copy-start | bytes 6148
  553.2 12.9 %copy-start.7 = (f32[16,1024]{1,0:T(8,128)S(1)}, f32[16,1024]{1,0:T(8,128)}, u32[]{:S(2)}) copy-start(f32[16,1024]{1,0:T(8,128)} %param.21) | copy-start | bytes 196612
  566.0 408.8 %reduce-scatter.2.cloned.1.call-start = ((), (), s32[]{:S(2)}) async-start(), calls=%async_computation.3 | async-start | bytes 655360 | tf_op jit(solution)/shard_map/reduce_scatter | solution.py:65
  974.8 3.5 collective-permute-start
  979.3 4.8 collective-permute-start.1
  984.1 5.4 collective-permute-start.2
  989.5 3.9 collective-permute-start.3
  993.4 10.0 collective-permute-start.4
Sparse Core Ops, SparseCore 0:
  25.8 143.2 all-reduce.4
  281.2 145.1 all-reduce.8
  566.2 148.1 all-reduce.6
  954.0 20.8 reduce-scatter.1
